TPU v7x, 256 devices: a whole 4x4x8 slice. The times are simulated.
256 devices in a mesh: dp: 4 (over x), shard: 64 (over y, z, core).
Axes of the slice: x: 4, y: 4, z: 8, core: 2. Of those that a mesh axis runs over, the one named last changes fastest.
Arguments:
- grad_partial: bfloat16 [4, 16, 512, 14336], P('dp', None, 'shard'), may hold values from -6 to 6
- second_moment: float32 [16, 512, 14336], P(None, 'shard', 'dp'), may hold values from 0.002 to 3, as said below
- params: bfloat16 [16, 512, 14336], P(None, 'shard', 'dp'), may hold values from -6 to 6
- left_roots: bfloat16 [4, 64, 3, 512, 512], P('dp', 'shard'), may hold values from -1 to 4, as said below
- right_roots: bfloat16 [4, 64, 3, 512, 512], P('dp', 'shard'), may hold values from -1 to 4, as said below
- owners: int32 [4, 112, 1], replicated, may hold values from 0 to 63; in each aligned block of 112 rows (0 to 111, 112 to 223, ..., all dimensions but the last counted through in order) at most 3 rows name the same one
Outputs:
- updated: bfloat16 [16, 512, 14336], P(None, 'shard')
Inputs may be any that keep to these rules, and one draw needn't show every extreme that they name: `second_moment`: second-moment estimates, positive. `left_roots`: symmetric factors. `right_roots`: symmetric factors. `owners`: in each group no owner is named by more than 3 blocks, a bound that some block reaches.
All inputs are finite; a program needn't handle non-finite values.
Results may differ from a plain program's by a relative error of at most 0.015.
Values may be sent and summed in bfloat16 or wider, within the bound.
A program may use at most 64 MiB of HBM per device.

v0:
```python
import functools
import jax
import jax.numpy as jnp
from jax import lax
from jax.experimental import pallas as pl
from jax.experimental.pallas import tpu as pltpu
from jax.sharding import PartitionSpec as P

BETA2 = 0.95
EPS_ADAM = 1e-08
EPS_NORM = 1e-06
STEP_RATE = 0.5
NY, NZ, NC = 4, 8, 2
LANES = 128
MESH = pl.DeviceIdType.MESH
F32, BF16 = jnp.float32, jnp.bfloat16


def wait_bytes(ref, sem):
    pltpu.make_async_copy(ref, ref, sem).wait()


def kernel(
    gp, sm, pr, lr, rr, ow, out,
    own, mid, far, comb, near, smv, prv, lv, rv, gf, acc,
    sel, selt, outgoing, incoming, half, prec, steps, returned, mine,
    nsrc, nz, nmid, npl,
    load_sem, rs_send, rs_recv, in_send, in_recv, ret_send, ret_recv,
    ag_send, ag_recv, n_send, n_recv, met,
):
    brows, bcols, pieces = own.shape[0], own.shape[1], own.shape[2]
    hb = brows // 2
    nb = brows * bcols
    shards, slots, rdev = outgoing.shape[1], outgoing.shape[2], outgoing.shape[3]
    bsize = lv.shape[1]
    d = lax.axis_index("dp")
    me = lax.axis_index("shard")
    y, z, c = me // (NZ * NC), (me // NC) % NZ, me % NC
    up, dn, op = (d + 1) % 4, (d + 3) % 4, (d + 2) % 4
    lo, hi = pl.ds(0, hb), pl.ds(hb, hb)

    def cols(group):
        return pl.ds(group * bcols, bcols)

    def peer(dy, dz, dc):
        return (((y + dy) % NY) * NZ + (z + dz) % NZ) * NC + (c + dc) % NC

    def for_peers(act):
        def outer(i, carry):
            plane = i // (NZ - 1)
            act(peer(plane // NC, 1 + i % (NZ - 1), plane % NC))
            return carry

        def inner(i, carry):
            act(peer(i // NC, 0, i % NC))
            return carry

        lax.fori_loop(0, (NZ - 1) * NY * NC, outer, 0)
        lax.fori_loop(1, NY * NC, inner, 0)

    bits = (shards - 1).bit_length()
    flips = [me + (1 - 2 * ((me // 2**k) % 2)) * 2**k for k in range(bits)]
    barrier = pltpu.get_barrier_semaphore()
    for other in (up, dn):
        pl.semaphore_signal(barrier, 1, device_id=(other, me), device_id_type=MESH)
    for other in flips:
        pl.semaphore_signal(barrier, 1, device_id=(d, other), device_id_type=MESH)

    def spread_barrier(rounds):
        for k in rounds:
            pl.semaphore_signal(met.at[k], 1, device_id=(d, flips[k]), device_id_type=MESH)
            pl.semaphore_wait(met.at[k], 1)

    loads = [
        (gp.at[lo, cols(up)], mid.at[0]),
        (gp.at[hi, cols(dn)], mid.at[1]),
        (gp.at[:, cols(d)], own),
        (sm, smv),
        (lr, lv),
        (rr, rv),
        (pr, prv),
    ]
    loads = [pltpu.make_async_copy(a, b, load_sem.at[i]) for i, (a, b) in enumerate(loads)]
    for load in loads:
        load.start()

    pl.semaphore_wait(barrier, 2 + bits)

    def rs(p, kind):
        src, dst, to = {
            "a": (gp.at[lo, cols(op), p], far.at[p, 0], up),
            "b": (gp.at[hi, cols(op), p], far.at[p, 1], dn),
            "c": (gp.at[hi, cols(up), p], near.at[p, 1], up),
            "d": (gp.at[lo, cols(dn), p], near.at[p, 2], dn),
            "e": (comb.at[p, 0], near.at[p, 0], up),
            "f": (comb.at[p, 1], near.at[p, 3], dn),
        }[kind]
        n = "abcdef".index(kind)
        return pltpu.make_async_remote_copy(
            src, dst, rs_send.at[p, n], rs_recv.at[p, n], device_id=(to, me), device_id_type=MESH
        )

    def start(p, kinds):
        if p < pieces:
            for kind in kinds:
                rs(p, kind).start()

    def combine(p):
        for h, kind in enumerate("ab"):
            rs(p, kind).wait_recv()

            def add(r, carry, h=h):
                s = mid[h, r, :, p].astype(F32) + far[p, h, r].astype(F32)
                comb[p, h, r] = s.astype(BF16)
                return carry

            lax.fori_loop(0, hb, add, 0)
            rs(p, "ef"[h]).start()

    def exchange(src, dst, p, send, recv):
        def act(t):
            pltpu.make_async_remote_copy(
                src.at[p, t], dst.at[p, me], send.at[p], recv.at[p], device_id=(d, t), device_id_type=MESH
            ).start()

        for_peers(act)
        pltpu.make_async_copy(src.at[p, me], dst.at[p, me], recv.at[p]).start()

    def finish(p):
        for kind in "cdef":
            rs(p, kind).wait_recv()
        for h in range(2):

            def one(r, carry, h=h):
                b = h * hb + r
                g = own[b, :, p].astype(F32) + near[p, h, r].astype(F32)
                gf[b] = g + near[p, 2 + h, r].astype(F32)
                return carry

            lax.fori_loop(0, hb, one, 0)
        blocks = gf[...].reshape(wide, LANES).astype(BF16)

        def pick(m, carry):
            got = jnp.dot(sel[pl.ds(m * mrows, mrows), :], blocks, preferred_element_type=F32)
            outgoing[p, pl.ds(m * 8, 8)] = got.reshape(8, slots, rdev, LANES).astype(BF16)
            return carry

        lax.fori_loop(0, shards // 8, pick, 0)
        exchange(outgoing, incoming, p, in_send, in_recv)

        def norms(b, carry):
            g = gf[b]
            vnew = BETA2 * smv[b, :, p] + (1.0 - BETA2) * g * g
            adam = g / (jnp.sqrt(vnew) + EPS_ADAM)
            acc[b] = adam * adam if p == 0 else acc[b] + adam * adam
            return carry

        lax.fori_loop(0, brows, norms, 0)

    start(0, "abcd")
    start(1, "ab")
    spread_barrier(range(0, bits // 2))
    table = ow[d].astype(F32)
    b0 = lax.broadcasted_iota(jnp.int32, (nb, nb), 0)
    b1 = lax.broadcasted_iota(jnp.int32, (nb, nb), 1)
    rows = jnp.broadcast_to(table, (nb, nb))
    column = jnp.sum(jnp.where(b0 == b1, rows, 0.0), axis=1, keepdims=True)
    same = jnp.where(rows == column, 1.0, 0.0)
    rank = jnp.sum(jnp.where(b0 < b1, same, 0.0), axis=0, keepdims=True)
    target = table * float(slots) + rank
    wide = nb * rdev
    e0 = lax.broadcasted_iota(jnp.int32, (nb, wide), 0) * rdev
    e1 = lax.broadcasted_iota(jnp.int32, (nb, wide), 1)
    spread = jnp.where((e1 >= e0) & (e1 < e0 + rdev), 1.0, 0.0).astype(BF16)
    wide_target = jnp.dot(
        jnp.broadcast_to(target, (8, nb)).astype(BF16), spread, preferred_element_type=F32
    )[0:1]
    l1 = lax.broadcasted_iota(jnp.int32, (1, wide), 1)
    wide_target = wide_target.astype(jnp.int32) * rdev + l1 % rdev
    t0 = lax.broadcasted_iota(jnp.int32, (wide, nb), 0)
    t1 = lax.broadcasted_iota(jnp.int32, (wide, nb), 1) * rdev
    tall = jnp.where((t0 >= t1) & (t0 < t1 + rdev), jnp.broadcast_to(target, (wide, nb)), 0.0)
    s0 = lax.broadcasted_iota(jnp.int32, (wide, 1), 0)
    tall_target = jnp.sum(tall, axis=1, keepdims=True).astype(jnp.int32) * rdev + s0 % rdev
    total_rows = shards * slots * rdev
    mrows = 8 * slots * rdev

    def fill(m, carry):
        r = lax.broadcasted_iota(jnp.int32, (mrows, wide), 0) + m * mrows
        sel[pl.ds(m * mrows, mrows), :] = jnp.where(r == wide_target, 1.0, 0.0).astype(BF16)
        return carry

    lax.fori_loop(0, total_rows // mrows, fill, 0)

    for load in loads[:2]:
        load.wait()
    for p in range(pieces + 1):
        if p < pieces:
            combine(p)
            start(p + 1, "cd")
            start(p + 2, "ab")
        if p == 0:
            spread_barrier(range(bits // 2, bits))
            for load in loads[2:4]:
                load.wait()
        if p > 0:
            finish(p - 1)

    sums = jnp.sum(jnp.sum(acc[...].reshape(nb, rdev, LANES), axis=1), axis=1, keepdims=True)
    n0 = lax.broadcasted_iota(jnp.int32, (nb, LANES), 0)
    n1 = lax.broadcasted_iota(jnp.int32, (nb, LANES), 1)
    spots = jnp.where(n0 == n1, jnp.broadcast_to(sums, (nb, LANES)), 0.0)
    nsrc[...] = jnp.sum(spots.reshape(nb // 8, 8, LANES), axis=0)
    for i in range(1, NZ):
        pltpu.make_async_remote_copy(
            nsrc, nz.at[z], n_send.at[0], n_recv.at[0], device_id=(d, peer(0, i, 0)), device_id_type=MESH
        ).start()
    pltpu.make_async_copy(nsrc, nz.at[z], n_recv.at[0]).start()

    for m in range(total_rows // 512):
        r = lax.broadcasted_iota(jnp.int32, (wide, 512), 1) + m * 512
        selt[:, m * 512 : (m + 1) * 512] = jnp.where(r == tall_target, 1.0, 0.0).astype(BF16)

    for load in loads[4:]:
        load.wait()

    def multiply(p):
        wait_bytes(incoming.at[p], in_recv.at[p])
        for k in range(slots):
            g = incoming[p, :, k].astype(F32).reshape(bsize, LANES).astype(BF16)
            half[k, :, p * LANES : (p + 1) * LANES] = jnp.dot(
                lv[k], g, preferred_element_type=F32
            ).astype(BF16)

    for p in range(pieces - 1):
        multiply(p)
    cut = (pieces - 1) * LANES
    for k in range(slots):
        prec[k] = jnp.dot(half[k, :, :cut], rv[k, :cut, :], preferred_element_type=F32)

    wait_bytes(nz, n_recv.at[0])
    nmid[...] = jnp.sum(nz[...], axis=0)
    for i in range(1, NY * NC):
        pltpu.make_async_remote_copy(
            nmid, npl.at[y * NC + c], n_send.at[1], n_recv.at[1],
            device_id=(d, peer(i // NC, 0, i % NC)), device_id_type=MESH,
        ).start()
    pltpu.make_async_copy(nmid, npl.at[y * NC + c], n_recv.at[1]).start()

    multiply(pieces - 1)
    squares = []
    for k in range(slots):
        total = jnp.zeros((1, bsize), F32)
        for r in range(0, bsize, LANES):
            x = prec[k, r : r + LANES] + jnp.dot(
                half[k, r : r + LANES, cut:], rv[k, cut:, :], preferred_element_type=F32
            )
            prec[k, r : r + LANES] = x
            total += jnp.sum(x * x, axis=0, keepdims=True)
        squares.append(jnp.sum(total, axis=1, keepdims=True))

    wait_bytes(npl, n_recv.at[1])
    totals = jnp.sum(jnp.sum(npl[...], axis=0), axis=0, keepdims=True)[:, :nb]
    scales = []
    for k in range(slots):
        here = (me * slots + k).astype(F32)
        adam_sq = jnp.sum(jnp.where(target == here, totals, 0.0), axis=1, keepdims=True)
        scales.append(jnp.sqrt(adam_sq) / (jnp.sqrt(squares[k]) + EPS_NORM))

    for p in range(pieces):
        for k in range(slots):
            x = prec[k, :, p * LANES : (p + 1) * LANES] * scales[k]
            steps[p, :, k] = x.reshape(shards, rdev, LANES).astype(BF16)
        exchange(steps, returned, p, ret_send, ret_recv)

    def ag(p, n):
        src, rows, group, to = [
            (mine, lo, d, up),
            (mine, hi, d, dn),
            (mine, hi, d, up),
            (mine, lo, d, dn),
            (out, lo, dn, up),
            (out, hi, up, dn),
        ][n]
        dst = out.at[rows, cols(group), p]
        src = mine.at[p, rows] if src is mine else dst
        return pltpu.make_async_remote_copy(
            src, dst, ag_send.at[p, n], ag_recv.at[p, n], device_id=(to, me), device_id_type=MESH
        )

    def ag_arrived(p, n):
        rows, group = [(lo, dn), (hi, up), (hi, dn), (lo, up), (lo, op), (hi, op)][n]
        wait_bytes(out.at[rows, cols(group), p], ag_recv.at[p, n])

    keep = [
        pltpu.make_async_copy(mine.at[p], out.at[:, cols(d), p], load_sem.at[p]) for p in range(pieces)
    ]

    def forward(p):
        for n in (0, 1):
            ag_arrived(p, n)
            ag(p, 4 + n).start()

    for p in range(pieces):
        wait_bytes(returned.at[p], ret_recv.at[p])
        back = returned[p].astype(F32).reshape(total_rows, LANES).astype(BF16)
        placed = jnp.dot(selt[...], back, preferred_element_type=F32)
        placed = placed.reshape(brows, bcols, rdev, LANES)
        mine[p] = (prv[:, :, p].astype(F32) - STEP_RATE * placed).astype(BF16)
        for n in range(4):
            ag(p, n).start()
        keep[p].start()
        if p > 0:
            forward(p - 1)
    forward(pieces - 1)

    for p in range(pieces):
        for n in range(2, 6):
            ag_arrived(p, n)
        keep[p].wait()
        for n in range(6):
            ag(p, n).wait_send()
        for kind in "abcdef":
            rs(p, kind).wait_send()
        wait_bytes(outgoing.at[p, pl.ds(0, shards - 1)], in_send.at[p])
        wait_bytes(steps.at[p, pl.ds(0, shards - 1)], ret_send.at[p])
    wait_bytes(nz.at[pl.ds(0, NZ - 1)], n_send.at[0])
    wait_bytes(npl.at[pl.ds(0, NY * NC - 1)], n_send.at[1])


def body(grad_partial, second_moment, params, left_roots, right_roots, owners):
    shards = lax.axis_size("shard")
    brows, rdev, ffall = grad_partial.shape[1:]
    slots, bsize = left_roots.shape[2], left_roots.shape[3]
    ffgroup = second_moment.shape[2]
    bcols = ffgroup // bsize
    groups = ffall // ffgroup
    pieces = bsize // LANES
    hb = brows // 2
    wide = brows * bcols * rdev

    def tiles(x):
        n = x.shape[-1]
        x = x.reshape(brows, rdev, n // LANES, LANES).transpose(0, 2, 1, 3)
        return x.reshape(brows, n // bsize, pieces, rdev, LANES)

    hbm = pl.BlockSpec(memory_space=pl.ANY)
    vmem = pl.BlockSpec(memory_space=pltpu.VMEM)
    dma = pltpu.SemaphoreType.DMA
    tile = (rdev, LANES)
    out = pl.pallas_call(
        kernel,
        out_shape=jax.ShapeDtypeStruct((brows, groups * bcols, pieces) + tile, BF16),
        in_specs=[hbm] * 5 + [vmem],
        out_specs=hbm,
        scratch_shapes=[
            pltpu.VMEM((brows, bcols, pieces) + tile, BF16),
            pltpu.VMEM((2, hb, bcols, pieces) + tile, BF16),
            pltpu.VMEM((pieces, 2, hb, bcols) + tile, BF16),
            pltpu.VMEM((pieces, 2, hb, bcols) + tile, BF16),
            pltpu.VMEM((pieces, 4, hb, bcols) + tile, BF16),
            pltpu.VMEM((brows, bcols, pieces) + tile, F32),
            pltpu.VMEM((brows, bcols, pieces) + tile, BF16),
            pltpu.VMEM((slots, bsize, bsize), BF16),
            pltpu.VMEM((slots, bsize, bsize), BF16),
            pltpu.VMEM((brows, bcols) + tile, F32),
            pltpu.VMEM((brows, bcols) + tile, F32),
            pltpu.VMEM((shards * slots * rdev, wide), BF16),
            pltpu.VMEM((wide, shards * slots * rdev), BF16),
            pltpu.VMEM((pieces, shards, slots) + tile, BF16),
            pltpu.VMEM((pieces, shards, slots) + tile, BF16),
            pltpu.VMEM((slots, bsize, bsize), BF16),
            pltpu.VMEM((slots, bsize, bsize), F32),
            pltpu.VMEM((pieces, shards, slots) + tile, BF16),
            pltpu.VMEM((pieces, shards, slots) + tile, BF16),
            pltpu.VMEM((pieces, brows, bcols) + tile, BF16),
            pltpu.VMEM((8, LANES), F32),
            pltpu.VMEM((NZ, 8, LANES), F32),
            pltpu.VMEM((8, LANES), F32),
            pltpu.VMEM((NY * NC, 8, LANES), F32),
            dma((7,)),
            dma((pieces, 6)),
            dma((pieces, 6)),
            dma((pieces,)),
            dma((pieces,)),
            dma((pieces,)),
            dma((pieces,)),
            dma((pieces, 6)),
            dma((pieces, 6)),
            dma((2,)),
            dma((2,)),
            pltpu.SemaphoreType.REGULAR(((shards - 1).bit_length(),)),
        ],
        compiler_params=pltpu.CompilerParams(
            collective_id=0, has_side_effects=True, vmem_limit_bytes=60 * 2**20
        ),
    )(
        tiles(grad_partial[0]),
        tiles(second_moment),
        tiles(params),
        left_roots[0, 0],
        right_roots[0, 0],
        owners.transpose(0, 2, 1),
    )
    out = out.reshape(brows, ffall // LANES, rdev, LANES).transpose(0, 2, 1, 3)
    return out.reshape(brows, rdev, ffall)


def solution(mesh):
    return jax.shard_map(
        body,
        mesh=mesh,
        in_specs=(
            P("dp", None, "shard", None),
            P(None, "shard", "dp"),
            P(None, "shard", "dp"),
            P("dp", "shard", None, None, None),
            P("dp", "shard", None, None, None),
            P(),
        ),
        out_specs=P(None, "shard", None),
        check_vma=False,
    )
```

profile of v0, /device:TPU:1, one launch (start us, length us, event | category | flops | bytes accessed | tf_op | source)
XLA Modules:
  0.0 121.4 jit_solution(1269941362965545167)
XLA Ops:
  0.0 117.1 %shard_map.64 = bf16[16,28,4,8,128]{4,3,2,1,0:T(8,128)(2,1)} custom-call(bf16[16,28,4,8,128]{4,3,2,1,0:T(8,128)(2,1)} %bitcast.24, f32[16,7,4,8,128]{4,3,2,1,0:T(8,128)} %bitcast.25, bf16[16,7,4,8,128]{4,3,2,1,0:T(8,128)(2,1)} %bitcast.28, bf16[3,512,512]{2,1,0:T(8,128)(2,1)} %bitcast.26, bf16[3,512,512]{2,1,0:T(8,128)(2,1)} %bitcast.27, s32[4,1,112]{2,1,0:T(1,128)} %bitcast.29), custom_call_target="tpu_custom_call" | custom-call | tf_op jit(solution)/shard_map/pallas_call | solution.py:351
  117.2 4.2 %copy.8 = bf16[16,8,14336]{2,1,0:T(8,128)(2,1)} copy(bf16[16,8,14336]{2,1,0:T(8,128)(2,1)} %bitcast.23) | data formatting | bytes 7340032
where the time goes:
time: 121 us
  Pallas kernels  117 us (97%)
  local copies, waits for them, and re-layouts  4.2 us (3%)
    pallas_call x1, Pallas kernels, body(): pl.pallas_call(kernel, out_shape=jax.ShapeDtypeStruct((brows, groups * bc...  117 us
    unnamed x1, local copies, waits for them, and re-layouts  4.2 us

commit v1 on v0

--- a/solution.py
+++ b/solution.py
@@ -38,6 +38,7 @@
     y, z, c = me // (NZ * NC), (me // NC) % NZ, me % NC
     up, dn, op = (d + 1) % 4, (d + 3) % 4, (d + 2) % 4
     lo, hi = pl.ds(0, hb), pl.ds(hb, hb)
+    last = pieces - 1
 
     def cols(group):
         return pl.ds(group * bcols, bcols)
@@ -58,18 +59,25 @@
         lax.fori_loop(0, (NZ - 1) * NY * NC, outer, 0)
         lax.fori_loop(1, NY * NC, inner, 0)
 
-    bits = (shards - 1).bit_length()
-    flips = [me + (1 - 2 * ((me // 2**k) % 2)) * 2**k for k in range(bits)]
+    zh = NZ // 4
+    digits = [
+        [peer(i, 0, 0) for i in range(1, NY)],
+        [(y * NZ + z // 4 * 4 + (z + i) % 4) * NC + c for i in range(1, 4)],
+        [
+            (y * NZ + (z // 4 + i // NC) % zh * 4 + z % 4) * NC + (c + i % NC) % NC
+            for i in range(1, zh * NC)
+        ],
+    ]
     barrier = pltpu.get_barrier_semaphore()
     for other in (up, dn):
         pl.semaphore_signal(barrier, 1, device_id=(other, me), device_id_type=MESH)
-    for other in flips:
+    for other in sum(digits, []):
         pl.semaphore_signal(barrier, 1, device_id=(d, other), device_id_type=MESH)
 
-    def spread_barrier(rounds):
-        for k in rounds:
-            pl.semaphore_signal(met.at[k], 1, device_id=(d, flips[k]), device_id_type=MESH)
-            pl.semaphore_wait(met.at[k], 1)
+    def spread_barrier(k):
+        for other in digits[k]:
+            pl.semaphore_signal(met.at[k], 1, device_id=(d, other), device_id_type=MESH)
+        pl.semaphore_wait(met.at[k], len(digits[k]))
 
     loads = [
         (gp.at[lo, cols(up)], mid.at[0]),
@@ -84,7 +92,7 @@
     for load in loads:
         load.start()
 
-    pl.semaphore_wait(barrier, 2 + bits)
+    pl.semaphore_wait(barrier, 2 + len(sum(digits, [])))
 
     def rs(p, kind):
         src, dst, to = {
@@ -117,14 +125,21 @@
             lax.fori_loop(0, hb, add, 0)
             rs(p, "ef"[h]).start()
 
-    def exchange(src, dst, p, send, recv):
+    def exchange(src, dst, p, first, count, send, recv):
+        which = pl.ds(first, count)
+
         def act(t):
             pltpu.make_async_remote_copy(
-                src.at[p, t], dst.at[p, me], send.at[p], recv.at[p], device_id=(d, t), device_id_type=MESH
+                src.at[p, t, which], dst.at[p, me, which], send, recv, device_id=(d, t), device_id_type=MESH
             ).start()
 
         for_peers(act)
-        pltpu.make_async_copy(src.at[p, me], dst.at[p, me], recv.at[p]).start()
+        pltpu.make_async_copy(src.at[p, me, which], dst.at[p, me, which], recv).start()
+
+    def fill(m, carry):
+        r = lax.broadcasted_iota(jnp.int32, (mrows, wide), 0) + m * mrows
+        sel[pl.ds(m * mrows, mrows), :] = jnp.where(r == wide_target, 1.0, 0.0).astype(BF16)
+        return carry
 
     def finish(p):
         for kind in "cdef":
@@ -146,7 +161,11 @@
             return carry
 
         lax.fori_loop(0, shards // 8, pick, 0)
-        exchange(outgoing, incoming, p, in_send, in_recv)
+        if p < last:
+            exchange(outgoing, incoming, p, 0, slots, in_send.at[p], in_recv.at[p])
+        else:
+            for k in range(slots):
+                exchange(outgoing, incoming, p, k, 1, in_send.at[p], in_recv.at[p + k])
 
         def norms(b, carry):
             g = gf[b]
@@ -159,7 +178,7 @@
 
     start(0, "abcd")
     start(1, "ab")
-    spread_barrier(range(0, bits // 2))
+    spread_barrier(0)
     table = ow[d].astype(F32)
     b0 = lax.broadcasted_iota(jnp.int32, (nb, nb), 0)
     b1 = lax.broadcasted_iota(jnp.int32, (nb, nb), 1)
@@ -185,13 +204,6 @@
     total_rows = shards * slots * rdev
     mrows = 8 * slots * rdev
 
-    def fill(m, carry):
-        r = lax.broadcasted_iota(jnp.int32, (mrows, wide), 0) + m * mrows
-        sel[pl.ds(m * mrows, mrows), :] = jnp.where(r == wide_target, 1.0, 0.0).astype(BF16)
-        return carry
-
-    lax.fori_loop(0, total_rows // mrows, fill, 0)
-
     for load in loads[:2]:
         load.wait()
     for p in range(pieces + 1):
@@ -200,56 +212,70 @@
             start(p + 1, "cd")
             start(p + 2, "ab")
         if p == 0:
-            spread_barrier(range(bits // 2, bits))
+            spread_barrier(1)
+            lax.fori_loop(0, total_rows // mrows, fill, 0)
             for load in loads[2:4]:
                 load.wait()
         if p > 0:
             finish(p - 1)
 
+    def sum_z(n):
+        for i in range(1, NZ):
+            pltpu.make_async_remote_copy(
+                nsrc.at[n], nz.at[n, z], n_send.at[n, 0], n_recv.at[n, 0],
+                device_id=(d, peer(0, i, 0)), device_id_type=MESH,
+            ).start()
+        pltpu.make_async_copy(nsrc.at[n], nz.at[n, z], n_recv.at[n, 0]).start()
+
+    def sum_plane(n):
+        wait_bytes(nz.at[n], n_recv.at[n, 0])
+        nmid[n] = jnp.sum(nz[n], axis=0)
+        for i in range(1, NY * NC):
+            pltpu.make_async_remote_copy(
+                nmid.at[n], npl.at[n, y * NC + c], n_send.at[n, 1], n_recv.at[n, 1],
+                device_id=(d, peer(i // NC, 0, i % NC)), device_id_type=MESH,
+            ).start()
+        pltpu.make_async_copy(nmid.at[n], npl.at[n, y * NC + c], n_recv.at[n, 1]).start()
+
+    def summed(n):
+        wait_bytes(npl.at[n], n_recv.at[n, 1])
+        return jnp.sum(jnp.sum(npl[n], axis=0), axis=0, keepdims=True)[:, :nb]
+
     sums = jnp.sum(jnp.sum(acc[...].reshape(nb, rdev, LANES), axis=1), axis=1, keepdims=True)
     n0 = lax.broadcasted_iota(jnp.int32, (nb, LANES), 0)
     n1 = lax.broadcasted_iota(jnp.int32, (nb, LANES), 1)
     spots = jnp.where(n0 == n1, jnp.broadcast_to(sums, (nb, LANES)), 0.0)
-    nsrc[...] = jnp.sum(spots.reshape(nb // 8, 8, LANES), axis=0)
-    for i in range(1, NZ):
-        pltpu.make_async_remote_copy(
-            nsrc, nz.at[z], n_send.at[0], n_recv.at[0], device_id=(d, peer(0, i, 0)), device_id_type=MESH
-        ).start()
-    pltpu.make_async_copy(nsrc, nz.at[z], n_recv.at[0]).start()
-
-    for m in range(total_rows // 512):
-        r = lax.broadcasted_iota(jnp.int32, (wide, 512), 1) + m * 512
-        selt[:, m * 512 : (m + 1) * 512] = jnp.where(r == tall_target, 1.0, 0.0).astype(BF16)
+    nsrc[0] = jnp.sum(spots.reshape(nb // 8, 8, LANES), axis=0)
+    sum_z(0)
 
     for load in loads[4:]:
         load.wait()
 
-    def multiply(p):
+    def multiply(p, k):
+        g = incoming[p, :, k].astype(F32).reshape(bsize, LANES).astype(BF16)
+        got = jnp.dot(lv[k], g, preferred_element_type=F32)
+        half[k, :, p * LANES : (p + 1) * LANES] = got.astype(BF16)
+
+    for p in range(last):
         wait_bytes(incoming.at[p], in_recv.at[p])
         for k in range(slots):
-            g = incoming[p, :, k].astype(F32).reshape(bsize, LANES).astype(BF16)
-            half[k, :, p * LANES : (p + 1) * LANES] = jnp.dot(
-                lv[k], g, preferred_element_type=F32
-            ).astype(BF16)
-
-    for p in range(pieces - 1):
-        multiply(p)
-    cut = (pieces - 1) * LANES
+            multiply(p, k)
+    cut = last * LANES
     for k in range(slots):
         prec[k] = jnp.dot(half[k, :, :cut], rv[k, :cut, :], preferred_element_type=F32)
 
-    wait_bytes(nz, n_recv.at[0])
-    nmid[...] = jnp.sum(nz[...], axis=0)
-    for i in range(1, NY * NC):
-        pltpu.make_async_remote_copy(
-            nmid, npl.at[y * NC + c], n_send.at[1], n_recv.at[1],
-            device_id=(d, peer(i // NC, 0, i % NC)), device_id_type=MESH,
-        ).start()
-    pltpu.make_async_copy(nmid, npl.at[y * NC + c], n_recv.at[1]).start()
-
-    multiply(pieces - 1)
-    squares = []
+    def step(p, k):
+        x = prec[k, :, p * LANES : (p + 1) * LANES]
+        steps[p, :, k] = x.reshape(shards, rdev, LANES).astype(BF16)
+
+    def send_back(p, first, count):
+        exchange(steps, returned, p, first, count, ret_send.at[p], ret_recv.at[p])
+
+    early = min(2, pieces)
+    pnorms = jnp.zeros((1, nb), F32)
     for k in range(slots):
+        wait_bytes(incoming.at[last, :, k], in_recv.at[last + k])
+        multiply(last, k)
         total = jnp.zeros((1, bsize), F32)
         for r in range(0, bsize, LANES):
             x = prec[k, r : r + LANES] + jnp.dot(
@@ -257,21 +283,31 @@
             )
             prec[k, r : r + LANES] = x
             total += jnp.sum(x * x, axis=0, keepdims=True)
-        squares.append(jnp.sum(total, axis=1, keepdims=True))
-
-    wait_bytes(npl, n_recv.at[1])
-    totals = jnp.sum(jnp.sum(npl[...], axis=0), axis=0, keepdims=True)[:, :nb]
-    scales = []
-    for k in range(slots):
         here = (me * slots + k).astype(F32)
-        adam_sq = jnp.sum(jnp.where(target == here, totals, 0.0), axis=1, keepdims=True)
-        scales.append(jnp.sqrt(adam_sq) / (jnp.sqrt(squares[k]) + EPS_NORM))
-
+        pnorms += jnp.where(target == here, jnp.sum(total, axis=1, keepdims=True), 0.0)
+        if k == 0:
+            for p in range(early):
+                step(p, k)
+                send_back(p, 0, 1)
+    nsrc[1] = jnp.zeros((8, LANES), F32)
+    nsrc[1, 0:1, :nb] = pnorms
+    sum_z(1)
     for p in range(pieces):
-        for k in range(slots):
-            x = prec[k, :, p * LANES : (p + 1) * LANES] * scales[k]
-            steps[p, :, k] = x.reshape(shards, rdev, LANES).astype(BF16)
-        exchange(steps, returned, p, ret_send, ret_recv)
+        for k in range(1 if p < early else 0, slots):
+            step(p, k)
+        if p < early:
+            send_back(p, 1, slots - 1)
+        else:
+            send_back(p, 0, slots)
+        if p == 0:
+            sum_plane(0)
+            sum_plane(1)
+    for m in range(total_rows // 512):
+        r = lax.broadcasted_iota(jnp.int32, (wide, 512), 1) + m * 512
+        selt[:, m * 512 : (m + 1) * 512] = jnp.where(r == tall_target, 1.0, 0.0).astype(BF16)
+    scale = jnp.sqrt(summed(0)) / (jnp.sqrt(summed(1)) + EPS_NORM)
+    tall = jnp.where((t0 >= t1) & (t0 < t1 + rdev), jnp.broadcast_to(scale, (wide, nb)), 0.0)
+    tall_scale = jnp.sum(tall, axis=1, keepdims=True) * STEP_RATE
 
     def ag(p, n):
         src, rows, group, to = [
@@ -305,8 +341,8 @@
         wait_bytes(returned.at[p], ret_recv.at[p])
         back = returned[p].astype(F32).reshape(total_rows, LANES).astype(BF16)
         placed = jnp.dot(selt[...], back, preferred_element_type=F32)
-        placed = placed.reshape(brows, bcols, rdev, LANES)
-        mine[p] = (prv[:, :, p].astype(F32) - STEP_RATE * placed).astype(BF16)
+        placed = (placed * tall_scale).reshape(brows, bcols, rdev, LANES)
+        mine[p] = (prv[:, :, p].astype(F32) - placed).astype(BF16)
         for n in range(4):
             ag(p, n).start()
         keep[p].start()
@@ -324,8 +360,9 @@
             rs(p, kind).wait_send()
         wait_bytes(outgoing.at[p, pl.ds(0, shards - 1)], in_send.at[p])
         wait_bytes(steps.at[p, pl.ds(0, shards - 1)], ret_send.at[p])
-    wait_bytes(nz.at[pl.ds(0, NZ - 1)], n_send.at[0])
-    wait_bytes(npl.at[pl.ds(0, NY * NC - 1)], n_send.at[1])
+    for n in range(2):
+        wait_bytes(nz.at[n, pl.ds(0, NZ - 1)], n_send.at[n, 0])
+        wait_bytes(npl.at[n, pl.ds(0, NY * NC - 1)], n_send.at[n, 1])
 
 
 def body(grad_partial, second_moment, params, left_roots, right_roots, owners):
@@ -345,14 +382,15 @@
         return x.reshape(brows, n // bsize, pieces, rdev, LANES)
 
     hbm = pl.BlockSpec(memory_space=pl.ANY)
+    place = pl.BlockSpec(memory_space=pl.ANY)
     vmem = pl.BlockSpec(memory_space=pltpu.VMEM)
     dma = pltpu.SemaphoreType.DMA
     tile = (rdev, LANES)
     out = pl.pallas_call(
         kernel,
-        out_shape=jax.ShapeDtypeStruct((brows, groups * bcols, pieces) + tile, BF16),
+        out_shape=pltpu.VMEM((brows, groups * bcols, pieces) + tile, BF16),
         in_specs=[hbm] * 5 + [vmem],
-        out_specs=hbm,
+        out_specs=place,
         scratch_shapes=[
             pltpu.VMEM((brows, bcols, pieces) + tile, BF16),
             pltpu.VMEM((2, hb, bcols, pieces) + tile, BF16),
@@ -374,25 +412,25 @@
             pltpu.VMEM((pieces, shards, slots) + tile, BF16),
             pltpu.VMEM((pieces, shards, slots) + tile, BF16),
             pltpu.VMEM((pieces, brows, bcols) + tile, BF16),
-            pltpu.VMEM((8, LANES), F32),
-            pltpu.VMEM((NZ, 8, LANES), F32),
-            pltpu.VMEM((8, LANES), F32),
-            pltpu.VMEM((NY * NC, 8, LANES), F32),
+            pltpu.VMEM((2, 8, LANES), F32),
+            pltpu.VMEM((2, NZ, 8, LANES), F32),
+            pltpu.VMEM((2, 8, LANES), F32),
+            pltpu.VMEM((2, NY * NC, 8, LANES), F32),
             dma((7,)),
             dma((pieces, 6)),
             dma((pieces, 6)),
             dma((pieces,)),
-            dma((pieces,)),
+            dma((pieces - 1 + slots,)),
             dma((pieces,)),
             dma((pieces,)),
             dma((pieces, 6)),
             dma((pieces, 6)),
-            dma((2,)),
-            dma((2,)),
-            pltpu.SemaphoreType.REGULAR(((shards - 1).bit_length(),)),
+            dma((2, 2)),
+            dma((2, 2)),
+            pltpu.SemaphoreType.REGULAR((2,)),
         ],
         compiler_params=pltpu.CompilerParams(
-            collective_id=0, has_side_effects=True, vmem_limit_bytes=60 * 2**20
+            collective_id=0, has_side_effects=True, vmem_limit_bytes=59 * 2**20
         ),
     )(
         tiles(grad_partial[0]),

time: 121 us -> 113 us (0.934)
  Pallas kernels: 117 us -> 111 us
  local copies, waits for them, and re-layouts: 4.2 us -> 1.84 us
    pallas_call x1, Pallas kernels: 117 us -> 111 us  [body(): pl.pallas_call(kernel, out_shape=pltpu.VMEM((brows, groups * bcols, piece...]
    unnamed x1, local copies, waits for them, and re-layouts: 4.2 us -> 1.84 us
where the time goes in v1:
time: 113 us
  Pallas kernels  111 us (98%)
  local copies, waits for them, and re-layouts  1.84 us (2%)
    pallas_call x1, Pallas kernels, body(): pl.pallas_call(kernel, out_shape=pltpu.VMEM((brows, groups * bcols, piece...  111 us

profile of v1, /device:TPU:1, one launch (start us, length us, event | category | flops | bytes accessed | tf_op | source)
XLA Modules:
  0.0 113.3 jit_solution(9709844981593076458)
XLA Ops:
  0.0 111.5 %shard_map.64 = bf16[16,28,4,8,128]{4,3,2,1,0:T(8,128)(2,1)S(1)} custom-call(bf16[16,28,4,8,128]{4,3,2,1,0:T(8,128)(2,1)} %bitcast.24, f32[16,7,4,8,128]{4,3,2,1,0:T(8,128)} %bitcast.25, bf16[16,7,4,8,128]{4,3,2,1,0:T(8,128)(2,1)} %bitcast.28, bf16[3,512,512]{2,1,0:T(8,128)(2,1)} %bitcast.26, bf16[3,512,512]{2,1,0:T(8,128)(2,1)} %bitcast.27, ...), custom_call_target="tpu_custom_call" | custom-call | tf_op jit(solution)/shard_map/pallas_call | solution.py:389
  111.5 1.8 %copy.8 = bf16[16,8,14336]{2,1,0:T(8,128)(2,1)} copy(bf16[16,8,14336]{2,1,0:T(8,128)(2,1)S(1)} %bitcast.23) | data formatting | bytes 7340032

commit v2 on v1

--- a/solution.py
+++ b/solution.py
@@ -346,9 +346,7 @@
         for n in range(4):
             ag(p, n).start()
         keep[p].start()
-        if p > 0:
-            forward(p - 1)
-    forward(pieces - 1)
+        forward(p)
 
     for p in range(pieces):
         for n in range(2, 6):

time: 113 us -> 112 us (level); the launches traced: 113 us -> 111 us
  Pallas kernels: 111 us -> 109 us
    pallas_call x1, Pallas kernels: 111 us -> 109 us  [body(): pl.pallas_call(kernel, out_shape=pltpu.VMEM((brows, groups * bcols, piece...]
where the time goes in v2:
time: 112 us; the launch traced here: 111 us
  Pallas kernels  109 us (97%)
  local copies, waits for them, and re-layouts  1.84 us (2%)
    pallas_call x1, Pallas kernels, body(): pl.pallas_call(kernel, out_shape=pltpu.VMEM((brows, groups * bcols, piece...  109 us

profile of v2, /device:TPU:1, one launch (start us, length us, event | category | flops | bytes accessed | tf_op | source)
XLA Modules:
  0.0 111.0 jit_solution(17357268606557006277)
XLA Ops:
  0.0 109.2 %shard_map.64 = bf16[16,28,4,8,128]{4,3,2,1,0:T(8,128)(2,1)S(1)} custom-call(bf16[16,28,4,8,128]{4,3,2,1,0:T(8,128)(2,1)} %bitcast.24, f32[16,7,4,8,128]{4,3,2,1,0:T(8,128)} %bitcast.25, bf16[16,7,4,8,128]{4,3,2,1,0:T(8,128)(2,1)} %bitcast.28, bf16[3,512,512]{2,1,0:T(8,128)(2,1)} %bitcast.26, bf16[3,512,512]{2,1,0:T(8,128)(2,1)} %bitcast.27, ...), custom_call_target="tpu_custom_call" | custom-call | tf_op jit(solution)/shard_map/pallas_call | solution.py:387
  109.2 1.8 %copy.8 = bf16[16,8,14336]{2,1,0:T(8,128)(2,1)} copy(bf16[16,8,14336]{2,1,0:T(8,128)(2,1)S(1)} %bitcast.23) | data formatting | bytes 7340032

commit v3 on v2

--- a/solution.py
+++ b/solution.py
@@ -22,7 +22,7 @@
 
 def kernel(
     gp, sm, pr, lr, rr, ow, out,
-    own, mid, far, comb, near, smv, prv, lv, rv, gf, acc,
+    owv, own, mid, far, comb, near, smv, prv, lv, rv, gf, acc,
     sel, selt, outgoing, incoming, half, prec, steps, returned, mine,
     nsrc, nz, nmid, npl,
     load_sem, rs_send, rs_recv, in_send, in_recv, ret_send, ret_recv,
@@ -87,9 +87,10 @@
         (lr, lv),
         (rr, rv),
         (pr, prv),
+        (ow, owv),
     ]
     loads = [pltpu.make_async_copy(a, b, load_sem.at[i]) for i, (a, b) in enumerate(loads)]
-    for load in loads:
+    for load in loads[-1:] + loads[:-1]:
         load.start()
 
     pl.semaphore_wait(barrier, 2 + len(sum(digits, [])))
@@ -164,8 +165,8 @@
         if p < last:
             exchange(outgoing, incoming, p, 0, slots, in_send.at[p], in_recv.at[p])
         else:
-            for k in range(slots):
-                exchange(outgoing, incoming, p, k, 1, in_send.at[p], in_recv.at[p + k])
+            exchange(outgoing, incoming, p, 0, 1, in_send.at[p], in_recv.at[p])
+            exchange(outgoing, incoming, p, 1, slots - 1, in_send.at[p], in_recv.at[p + 1])
 
         def norms(b, carry):
             g = gf[b]
@@ -179,7 +180,8 @@
     start(0, "abcd")
     start(1, "ab")
     spread_barrier(0)
-    table = ow[d].astype(F32)
+    loads[-1].wait()
+    table = owv[d].astype(F32)
     b0 = lax.broadcasted_iota(jnp.int32, (nb, nb), 0)
     b1 = lax.broadcasted_iota(jnp.int32, (nb, nb), 1)
     rows = jnp.broadcast_to(table, (nb, nb))
@@ -206,6 +208,16 @@
 
     for load in loads[:2]:
         load.wait()
+    def multiply(p, k):
+        g = incoming[p, :, k].astype(F32).reshape(bsize, LANES).astype(BF16)
+        got = jnp.dot(lv[k], g, preferred_element_type=F32)
+        half[k, :, p * LANES : (p + 1) * LANES] = got.astype(BF16)
+
+    def multiply_all(p):
+        wait_bytes(incoming.at[p], in_recv.at[p])
+        for k in range(slots):
+            multiply(p, k)
+
     for p in range(pieces + 1):
         if p < pieces:
             combine(p)
@@ -216,6 +228,10 @@
             lax.fori_loop(0, total_rows // mrows, fill, 0)
             for load in loads[2:4]:
                 load.wait()
+        if p == pieces:
+            for load in loads[4:-1]:
+                load.wait()
+            multiply_all(0)
         if p > 0:
             finish(p - 1)
 
@@ -248,18 +264,8 @@
     nsrc[0] = jnp.sum(spots.reshape(nb // 8, 8, LANES), axis=0)
     sum_z(0)
 
-    for load in loads[4:]:
-        load.wait()
-
-    def multiply(p, k):
-        g = incoming[p, :, k].astype(F32).reshape(bsize, LANES).astype(BF16)
-        got = jnp.dot(lv[k], g, preferred_element_type=F32)
-        half[k, :, p * LANES : (p + 1) * LANES] = got.astype(BF16)
-
-    for p in range(last):
-        wait_bytes(incoming.at[p], in_recv.at[p])
-        for k in range(slots):
-            multiply(p, k)
+    for p in range(1, last):
+        multiply_all(p)
     cut = last * LANES
     for k in range(slots):
         prec[k] = jnp.dot(half[k, :, :cut], rv[k, :cut, :], preferred_element_type=F32)
@@ -274,7 +280,10 @@
     early = min(2, pieces)
     pnorms = jnp.zeros((1, nb), F32)
     for k in range(slots):
-        wait_bytes(incoming.at[last, :, k], in_recv.at[last + k])
+        if k == 0:
+            wait_bytes(incoming.at[last, :, 0], in_recv.at[last])
+        if k == 1:
+            wait_bytes(incoming.at[last, :, pl.ds(1, slots - 1)], in_recv.at[last + 1])
         multiply(last, k)
         total = jnp.zeros((1, bsize), F32)
         for r in range(0, bsize, LANES):
@@ -381,15 +390,15 @@
 
     hbm = pl.BlockSpec(memory_space=pl.ANY)
     place = pl.BlockSpec(memory_space=pl.ANY)
-    vmem = pl.BlockSpec(memory_space=pltpu.VMEM)
     dma = pltpu.SemaphoreType.DMA
     tile = (rdev, LANES)
     out = pl.pallas_call(
         kernel,
         out_shape=pltpu.VMEM((brows, groups * bcols, pieces) + tile, BF16),
-        in_specs=[hbm] * 5 + [vmem],
+        in_specs=[hbm] * 6,
         out_specs=place,
         scratch_shapes=[
+            pltpu.VMEM((groups, 1, brows * bcols), jnp.int32),
             pltpu.VMEM((brows, bcols, pieces) + tile, BF16),
             pltpu.VMEM((2, hb, bcols, pieces) + tile, BF16),
             pltpu.VMEM((pieces, 2, hb, bcols) + tile, BF16),
@@ -414,11 +423,11 @@
             pltpu.VMEM((2, NZ, 8, LANES), F32),
             pltpu.VMEM((2, 8, LANES), F32),
             pltpu.VMEM((2, NY * NC, 8, LANES), F32),
-            dma((7,)),
+            dma((8,)),
             dma((pieces, 6)),
             dma((pieces, 6)),
             dma((pieces,)),
-            dma((pieces - 1 + slots,)),
+            dma((pieces + 1,)),
             dma((pieces,)),
             dma((pieces,)),
             dma((pieces, 6)),

time: 112 us -> 111 us (level)
  no operation moved by 1% of the time
where the time goes in v3:
time: 111 us
  Pallas kernels  109 us (98%)
  local copies, waits for them, and re-layouts  1.84 us (2%)
    pallas_call x1, Pallas kernels, body(): pl.pallas_call(kernel, out_shape=pltpu.VMEM((brows, groups * bcols, piece...  109 us

profile of v3, /device:TPU:1, one launch (start us, length us, event | category | flops | bytes accessed | tf_op | source)
XLA Modules:
  0.0 110.9 jit_solution(2079111078050497045)
XLA Ops:
  0.0 109.1 %shard_map.64 = bf16[16,28,4,8,128]{4,3,2,1,0:T(8,128)(2,1)S(1)} custom-call(bf16[16,28,4,8,128]{4,3,2,1,0:T(8,128)(2,1)} %bitcast.24, f32[16,7,4,8,128]{4,3,2,1,0:T(8,128)} %bitcast.25, bf16[16,7,4,8,128]{4,3,2,1,0:T(8,128)(2,1)} %bitcast.28, bf16[3,512,512]{2,1,0:T(8,128)(2,1)} %bitcast.26, bf16[3,512,512]{2,1,0:T(8,128)(2,1)} %bitcast.27, ...), custom_call_target="tpu_custom_call" | custom-call | tf_op jit(solution)/shard_map/pallas_call | solution.py:395
  109.1 1.8 %copy.8 = bf16[16,8,14336]{2,1,0:T(8,128)(2,1)} copy(bf16[16,8,14336]{2,1,0:T(8,128)(2,1)S(1)} %bitcast.23) | data formatting | bytes 7340032

commit v4 on v3

--- a/solution.py
+++ b/solution.py
@@ -30,6 +30,7 @@
 ):
     brows, bcols, pieces = own.shape[0], own.shape[1], own.shape[2]
     hb = brows // 2
+    qb = hb // 2
     nb = brows * bcols
     shards, slots, rdev = outgoing.shape[1], outgoing.shape[2], outgoing.shape[3]
     bsize = lv.shape[1]
@@ -97,14 +98,18 @@
 
     def rs(p, kind):
         src, dst, to = {
-            "a": (gp.at[lo, cols(op), p], far.at[p, 0], up),
-            "b": (gp.at[hi, cols(op), p], far.at[p, 1], dn),
+            "a": (gp.at[pl.ds(0, qb), cols(op), p], far.at[p, 0, pl.ds(0, qb)], up),
+            "b": (gp.at[pl.ds(hb, qb), cols(op), p], far.at[p, 1, pl.ds(0, qb)], dn),
+            "g": (gp.at[pl.ds(qb, qb), cols(op), p], far.at[p, 0, pl.ds(qb, qb)], up),
+            "h": (gp.at[pl.ds(hb + qb, qb), cols(op), p], far.at[p, 1, pl.ds(qb, qb)], dn),
             "c": (gp.at[hi, cols(up), p], near.at[p, 1], up),
             "d": (gp.at[lo, cols(dn), p], near.at[p, 2], dn),
-            "e": (comb.at[p, 0], near.at[p, 0], up),
-            "f": (comb.at[p, 1], near.at[p, 3], dn),
+            "e": (comb.at[p, 0, pl.ds(0, qb)], near.at[p, 0, pl.ds(0, qb)], up),
+            "f": (comb.at[p, 1, pl.ds(0, qb)], near.at[p, 3, pl.ds(0, qb)], dn),
+            "i": (comb.at[p, 0, pl.ds(qb, qb)], near.at[p, 0, pl.ds(qb, qb)], up),
+            "j": (comb.at[p, 1, pl.ds(qb, qb)], near.at[p, 3, pl.ds(qb, qb)], dn),
         }[kind]
-        n = "abcdef".index(kind)
+        n = "abcdefghij".index(kind)
         return pltpu.make_async_remote_copy(
             src, dst, rs_send.at[p, n], rs_recv.at[p, n], device_id=(to, me), device_id_type=MESH
         )
@@ -115,7 +120,8 @@
                 rs(p, kind).start()
 
     def combine(p):
-        for h, kind in enumerate("ab"):
+        for n, kind in enumerate("abgh"):
+            h, first = n % 2, n // 2 * qb
             rs(p, kind).wait_recv()
 
             def add(r, carry, h=h):
@@ -123,8 +129,8 @@
                 comb[p, h, r] = s.astype(BF16)
                 return carry
 
-            lax.fori_loop(0, hb, add, 0)
-            rs(p, "ef"[h]).start()
+            lax.fori_loop(first, first + qb, add, 0)
+            rs(p, "efij"[n]).start()
 
     def exchange(src, dst, p, first, count, send, recv):
         which = pl.ds(first, count)
@@ -143,7 +149,7 @@
         return carry
 
     def finish(p):
-        for kind in "cdef":
+        for kind in "cdefij":
             rs(p, kind).wait_recv()
         for h in range(2):
 
@@ -177,8 +183,8 @@
 
         lax.fori_loop(0, brows, norms, 0)
 
-    start(0, "abcd")
-    start(1, "ab")
+    start(0, "abghcd")
+    start(1, "abgh")
     spread_barrier(0)
     loads[-1].wait()
     table = owv[d].astype(F32)
@@ -222,7 +228,7 @@
         if p < pieces:
             combine(p)
             start(p + 1, "cd")
-            start(p + 2, "ab")
+            start(p + 2, "abgh")
         if p == 0:
             spread_barrier(1)
             lax.fori_loop(0, total_rows // mrows, fill, 0)
@@ -363,7 +369,7 @@
         keep[p].wait()
         for n in range(6):
             ag(p, n).wait_send()
-        for kind in "abcdef":
+        for kind in "abcdefghij":
             rs(p, kind).wait_send()
         wait_bytes(outgoing.at[p, pl.ds(0, shards - 1)], in_send.at[p])
         wait_bytes(steps.at[p, pl.ds(0, shards - 1)], ret_send.at[p])
@@ -424,8 +430,8 @@
             pltpu.VMEM((2, 8, LANES), F32),
             pltpu.VMEM((2, NY * NC, 8, LANES), F32),
             dma((8,)),
-            dma((pieces, 6)),
-            dma((pieces, 6)),
+            dma((pieces, 10)),
+            dma((pieces, 10)),
             dma((pieces,)),
             dma((pieces + 1,)),
             dma((pieces,)),

time: 111 us -> 111 us (level)
  no operation moved by 1% of the time
where the time goes in v4:
time: 111 us
  Pallas kernels  109 us (98%)
  local copies, waits for them, and re-layouts  1.84 us (2%)
    pallas_call x1, Pallas kernels, body(): pl.pallas_call(kernel, out_shape=pltpu.VMEM((brows, groups * bcols, piece...  109 us

profile of v4, /device:TPU:1, one launch (start us, length us, event | category | flops | bytes accessed | tf_op | source)
XLA Modules:
  0.0 111.2 jit_solution(10871505800774295232)
XLA Ops:
  0.0 109.4 %shard_map.64 = bf16[16,28,4,8,128]{4,3,2,1,0:T(8,128)(2,1)S(1)} custom-call(bf16[16,28,4,8,128]{4,3,2,1,0:T(8,128)(2,1)} %bitcast.24, f32[16,7,4,8,128]{4,3,2,1,0:T(8,128)} %bitcast.25, bf16[16,7,4,8,128]{4,3,2,1,0:T(8,128)(2,1)} %bitcast.28, bf16[3,512,512]{2,1,0:T(8,128)(2,1)} %bitcast.26, bf16[3,512,512]{2,1,0:T(8,128)(2,1)} %bitcast.27, ...), custom_call_target="tpu_custom_call" | custom-call | tf_op jit(solution)/shard_map/pallas_call | solution.py:401
  109.4 1.8 %copy.8 = bf16[16,8,14336]{2,1,0:T(8,128)(2,1)} copy(bf16[16,8,14336]{2,1,0:T(8,128)(2,1)S(1)} %bitcast.23) | data formatting | bytes 7340032
